TPU v7x, 256 devices: a whole 4x4x8 slice. The times are simulated.
256 devices in a mesh: dom: 64 (over y, z, core), kv: 4 (over x).
Axes of the slice: x: 4, y: 4, z: 8, core: 2. Of those that a mesh axis runs over, the one named last changes fastest.
Arguments:
- node_feats: bfloat16 [32768, 128], P(('dom', 'kv')), may hold values from -11 to 11
- positions: float32 [3, 32768], P(None, ('dom', 'kv')), may hold values from 0 to 2304, as said below
- species: int32 [32768], P(('dom', 'kv')), may hold values from 0 to 1
- halo_rows: int32 [256, 64], P(('dom', 'kv')), may hold values from 0 to 127, as said below
- neighbours: int32 [32768, 32], P(('dom', 'kv')), may hold values from 0 to 191, as said below
- nbr_count: int32 [32768], P(('dom', 'kv')), may hold values from 16 to 32, as said below
- recip_vectors: int32 [3, 16384], replicated, may hold values from -13 to 13, as said below
- w_msg: bfloat16 [128, 128], replicated, may hold values from -0.5 to 0.5
- w_rad1: bfloat16 [8, 128], replicated, may hold values from -2 to 2
- w_rad2: bfloat16 [128, 256], replicated, may hold values from -0.5 to 0.5
- w_upd: bfloat16 [384, 128], replicated, may hold values from -0.3125 to 0.3125
- w_out: bfloat16 [128], replicated, may hold values from -0.5 to 0.5
- chi_table: float32 [2], replicated, may hold values from -1 to 1
- hard_table: float32 [2], replicated, may hold values from 0.5 to 2
Outputs:
- electroneg: float32 [32768], P(('dom', 'kv'))
- charges: float32 [32768], P(('dom', 'kv'))
Inputs may be any that keep to these rules, and one draw needn't show every extreme that they name: `halo_rows`: in each slab's row, 64 distinct local atom indices; the first 32 lie near the slab's lower face, the rest near its upper face. `neighbours`: an atom never lists its own local index. `nbr_count`: the first atom of every slab has all 32 slots live. `recip_vectors`: distinct nonzero triples. `positions`: atoms of slab s have first coordinate in [9 s, 9 (s + 1)), the other two in [0, 20).
All inputs are finite; a program needn't handle non-finite values.
Results may differ from a plain program's by a relative error of at most 0.003.
Values may be sent and summed in bfloat16 or wider, within the bound.
A program may use at most 128 MiB of HBM per device.

v0:
```python
import math
import jax
import jax.numpy as jnp
from jax import lax
from jax.sharding import PartitionSpec as P

ITERS = 4
slab_width = 9.0
side_length = 20.0
two_pi = 2.0 * math.pi
highest = lax.Precision.HIGHEST


def with_halo(block, sides, width):
    for axis, dim in sides:
        count = lax.axis_size(axis)
        forward = [(i, i + 1) for i in range(count - 1)]
        forward.append((count - 1, 0))
        backward = [(target, source) for source, target in forward]
        low = lax.ppermute(
            lax.slice_in_dim(block, block.shape[dim] - width, None, axis=dim), axis, forward
        )
        high = lax.ppermute(lax.slice_in_dim(block, 0, width, axis=dim), axis, backward)
        block = jnp.concatenate([low, block, high], axis=dim)
    return block


def wrapped(offset, length):
    return jnp.where(
        offset > 0.5 * length,
        offset - length,
        jnp.where(offset < -0.5 * length, offset + length, offset),
    )


def recip_setup(coords, triples, box_x, atoms_total):
    comp_x = triples[0].astype(jnp.float32)
    comp_y = triples[1].astype(jnp.float32)
    comp_z = triples[2].astype(jnp.float32)
    phase_arg = two_pi * (
        coords[0][:, None] * (comp_x / box_x)[None, :]
        + coords[1][:, None] * (comp_y / side_length)[None, :]
        + coords[2][:, None] * (comp_z / side_length)[None, :]
    )
    phase_table = jnp.concatenate([jnp.cos(phase_arg), jnp.sin(phase_arg)], axis=1)
    m_square = comp_x * comp_x + comp_y * comp_y + comp_z * comp_z
    weight = 16.0 / atoms_total * jnp.exp(-m_square / 400.0) / (1.0 + m_square / 16.0)
    return (phase_table, weight)


def message_layer(
    ext_proj,
    ext_pos,
    own_pos,
    own_feats,
    nbr_index,
    counts,
    kinds,
    w_rad1,
    w_rad2,
    w_upd,
    w_out,
    chi_table,
    box_x,
):
    atoms_dev, slot_count = nbr_index.shape
    channels = own_feats.shape[1]
    flat_index = nbr_index.reshape(-1)
    nbr_proj = jnp.take(ext_proj, flat_index, axis=0).reshape(atoms_dev, slot_count, channels)
    nbr_pos = jnp.take(ext_pos, flat_index, axis=1).reshape(3, atoms_dev, slot_count)
    displace = jnp.stack(
        [
            wrapped(nbr_pos[0] - own_pos[0][:, None], box_x),
            wrapped(nbr_pos[1] - own_pos[1][:, None], side_length),
            wrapped(nbr_pos[2] - own_pos[2][:, None], side_length),
        ]
    )
    distance = jnp.sqrt(jnp.sum(displace * displace, axis=0) + 0.25)
    unit_vec = displace / distance
    basis_count = w_rad1.shape[0]
    centres = 1.0 + 1.25 * jnp.arange(basis_count, dtype=jnp.float32)
    radial_basis = jnp.exp(-jnp.square((distance[:, :, None] - centres) / 1.25)).astype(
        jnp.bfloat16
    )
    hidden = jax.nn.silu(
        jnp.dot(radial_basis.reshape(-1, basis_count), w_rad1, preferred_element_type=jnp.float32)
    ).astype(jnp.bfloat16)
    radial = jnp.dot(hidden, w_rad2, preferred_element_type=jnp.float32).reshape(
        atoms_dev, slot_count, 2 * channels
    )
    live_mask = (jnp.arange(slot_count)[None, :] < counts[:, None]).astype(jnp.float32)
    radial = radial * live_mask[:, :, None]
    msg_scale = 1.0 / math.sqrt(slot_count)
    scalar_msg = jnp.sum(radial[:, :, :channels] * nbr_proj, axis=1) * msg_scale
    carried = radial[:, :, channels:] * nbr_proj
    vector_msg = jnp.sum(unit_vec[:, :, :, None] * carried[None], axis=2) * msg_scale
    vec_square = jnp.sum(vector_msg * vector_msg, axis=0)
    joined = jnp.concatenate(
        [scalar_msg, vec_square, own_feats.astype(jnp.float32)], axis=1
    ).astype(jnp.bfloat16)
    update = jax.nn.silu(jnp.dot(joined, w_upd, preferred_element_type=jnp.float32)).astype(
        jnp.bfloat16
    )
    one_hot = (kinds[:, None] == jnp.arange(chi_table.shape[0])[None, :]).astype(jnp.float32)
    return jnp.dot(update, w_out, preferred_element_type=jnp.float32) + jnp.sum(
        one_hot * chi_table[None, :], axis=1
    )


def squares(residual):
    return lax.psum(jnp.sum(residual * residual, axis=1), ("dom", "kv"))


def local(
    node_feats,
    positions,
    species,
    halo_rows,
    neighbours,
    nbr_count,
    recip_vectors,
    w_msg,
    w_rad1,
    w_rad2,
    w_upd,
    w_out,
    chi_table,
    hard_table,
):
    atoms_dev = node_feats.shape[0]
    halo_width = halo_rows.shape[1] // 2
    slab_count = lax.axis_size("dom") * lax.axis_size("kv")
    box_x = slab_count * slab_width
    atoms_total = atoms_dev * slab_count
    send_rows = halo_rows[0]
    packet_feats = jnp.take(node_feats, send_rows, axis=0)
    packet_pos = jnp.take(positions, send_rows, axis=1).T
    got_feats = with_halo(packet_feats, ((("dom", "kv"), 0),), halo_width)
    got_pos = with_halo(packet_pos, ((("dom", "kv"), 0),), halo_width)
    own_proj = jnp.dot(node_feats, w_msg, preferred_element_type=jnp.float32).astype(jnp.bfloat16)
    far_feats = jnp.concatenate([got_feats[:halo_width], got_feats[3 * halo_width :]], axis=0)
    far_proj = jnp.dot(far_feats, w_msg, preferred_element_type=jnp.float32).astype(jnp.bfloat16)
    ext_proj = jnp.concatenate([own_proj, far_proj], axis=0)
    ext_pos = jnp.concatenate(
        [positions, got_pos[:halo_width].T, got_pos[3 * halo_width :].T], axis=1
    )
    electroneg = message_layer(
        ext_proj,
        ext_pos,
        positions,
        node_feats,
        neighbours,
        nbr_count,
        species,
        w_rad1,
        w_rad2,
        w_upd,
        w_out,
        chi_table,
        box_x,
    )
    one_hot = (species[:, None] == jnp.arange(hard_table.shape[0])[None, :]).astype(jnp.float32)
    hardness = jnp.sum(one_hot * hard_table[None, :], axis=1)
    phase_table, weight = recip_setup(positions, recip_vectors, box_x, atoms_total)
    weight_pair = jnp.concatenate([weight, weight])
    right_side = jnp.stack([-electroneg, jnp.ones_like(electroneg)])
    solution = jnp.zeros_like(right_side)
    residual = right_side
    direction = right_side
    norm_now = squares(residual)
    for iteration in range(ITERS):
        partial_value = jnp.dot(
            direction, phase_table, precision=highest, preferred_element_type=jnp.float32
        )
        summed = lax.psum(partial_value, ("dom", "kv"))
        potential = lax.dot_general(
            summed * weight_pair,
            phase_table,
            (((1,), (1,)), ((), ())),
            precision=highest,
            preferred_element_type=jnp.float32,
        )
        applied = hardness * direction + potential
        curvature = lax.psum(jnp.sum(direction * applied, axis=1), ("dom", "kv"))
        step_size = norm_now / curvature
        solution = solution + step_size[:, None] * direction
        residual = residual - step_size[:, None] * applied
        if iteration + 1 < ITERS:
            norm_next = squares(residual)
            direction = residual + (norm_next / norm_now)[:, None] * direction
            norm_now = norm_next
    totals = lax.psum(jnp.sum(solution, axis=1), ("dom", "kv"))
    charges = solution[0] - totals[0] / totals[1] * solution[1]
    return (electroneg, charges)


def solution(mesh):
    return jax.shard_map(
        local,
        mesh=mesh,
        in_specs=(
            P(("dom", "kv"), None),
            P(None, ("dom", "kv")),
            P(("dom", "kv")),
            P(("dom", "kv"), None),
            P(("dom", "kv"), None),
            P(("dom", "kv")),
            P(),
            P(),
            P(),
            P(),
            P(),
            P(),
            P(),
            P(),
        ),
        out_specs=(P(("dom", "kv")), P(("dom", "kv"))),
        check_vma=False,
    )
```

profile of v0, /device:TPU:1, one launch (start us, length us, event | category | flops | bytes accessed | tf_op | source)
XLA Modules:
  0.0 1828.8 jit_solution(18002408356740054125)
XLA Ops:
  7.2 0.7 compare_and_fusion.2
  7.9 0.7 fusion.49
  8.6 1.4 gather_fusion.2
  10.0 2.1 collective-permute-start.2
  12.1 1.9 collective-permute-start.3
  14.1 0.8 copy.50
  14.8 0.6 gather_fusion
  15.6 3.1 collective-permute-start.1
  18.8 0.8 slice_bitcast_fusion.2
  19.6 0.7 compare_and_fusion
  20.3 0.8 copy.48
  21.3 0.9 convolution_convert_fusion
  22.2 0.7 fusion.35
  23.0 1.6 multiply_divide_fusion
  24.6 0.8 select_reduce_fusion
  25.4 33.0 %fusion.1 = (f32[128,16384]{1,0:T(8,128)}, f32[128,16384]{1,0:T(8,128)}) fusion(f32[16384]{0:T(1024)S(1)} %bitcast.46, f32[128]{0:T(128)S(1)} %get-tuple-element.32, f32[16384]{0:T(1024)S(1)} %bitcast.47, f32[128]{0:T(128)S(1)} %get-tuple-element.33, f32[16384]{0:T(1024)S(1)} %bitcast.45, f32[128]{0:T(128)S(1)} %get-tuple-element.31), kind=kLoop, calls=%fused_computation.7 | loop fusion | flops 12582912 | bytes 16975360 | tf_op jit(solution)/shard_map/cos | solution.py:45
  58.5 10.8 gather_fusion.1
  69.3 2.1 select_bitcast_fusion
  71.5 2.8 slice_reduce_fusion.2
  75.2 3.3 fusion.3
  78.5 3.9 broadcast_multiply_fusion
  82.7 12.1 gather_fusion.3
  94.9 3.3 fusion.2
  98.2 2.2 multiply_reduce_fusion
  100.5 0.3 fusion.6
  100.8 13.9 fusion.41
  114.8 253.6 %all-reduce.7.cloned.1.call-done = f32[2,32768]{1,0:T(2,128)} async-done(((f32[2,32768]{1,0:T(2,128)}), f32[2,32768]{1,0:T(2,128)}) %all-reduce.7.cloned.1.call-update) | async-done | bytes 262160 | tf_op jit(solution)/shard_map/psum | solution.py:175
  368.4 16.8 fusion.44
  385.2 77.9 %all-reduce.1 = (f32[2]{0:T(128)S(1)}, f32[2]{0:T(128)S(1)}) all-reduce(f32[2]{0:T(128)S(1)} %get-tuple-element.6, f32[2]{0:T(128)S(1)} %get-tuple-element.5), channel_id=1, replica_groups=mesh['dom'=64,'kv'=4] {'dom','kv'}, use_global_device_ids=true, to_apply=%region_6.7 | all-reduce | flops 4 | bytes 32 | tf_op jit(solution)/shard_map/psum | solution.py:111
  463.2 73.2 %psum.94 = f32[2]{0:T(128)S(1)} all-reduce(f32[2]{0:T(128)S(1)} %get-tuple-element.17), channel_id=1, replica_groups=mesh['dom'=64,'kv'=4] {'dom','kv'}, use_global_device_ids=true, to_apply=%region_12.13 | all-reduce | flops 2 | bytes 16 | tf_op jit(solution)/shard_map/psum | solution.py:111
  536.5 13.6 fusion.61
  550.2 245.8 %all-reduce.9.cloned.1.call-done = f32[2,32768]{1,0:T(2,128)} async-done(((f32[2,32768]{1,0:T(2,128)}), f32[2,32768]{1,0:T(2,128)}) %all-reduce.9.cloned.1.call-update) | async-done | bytes 262160 | tf_op jit(solution)/shard_map/psum | solution.py:175
  796.0 16.9 multiply_reduce_fusion.6
  812.9 77.4 %psum.96 = f32[2]{0:T(128)S(1)} all-reduce(f32[2]{0:T(128)S(1)} %get-tuple-element.37), channel_id=1, replica_groups=mesh['dom'=64,'kv'=4] {'dom','kv'}, use_global_device_ids=true, to_apply=%region_15.16 | all-reduce | flops 2 | bytes 16 | tf_op jit(solution)/shard_map/psum | solution.py:184
  890.5 73.4 %psum.97 = f32[2]{0:T(128)S(1)} all-reduce(f32[2]{0:T(128)S(1)} %get-tuple-element.15), channel_id=1, replica_groups=mesh['dom'=64,'kv'=4] {'dom','kv'}, use_global_device_ids=true, to_apply=%region_17.18 | all-reduce | flops 2 | bytes 16 | tf_op jit(solution)/shard_map/psum | solution.py:111
  964.1 13.6 fusion.60
  977.7 245.9 %all-reduce.11.cloned.1.call-done = f32[2,32768]{1,0:T(2,128)} async-done(((f32[2,32768]{1,0:T(2,128)}), f32[2,32768]{1,0:T(2,128)}) %all-reduce.11.cloned.1.call-update) | async-done | bytes 262160 | tf_op jit(solution)/shard_map/psum | solution.py:175
  1223.7 17.0 multiply_reduce_fusion.4
  1240.7 77.4 %psum.99 = f32[2]{0:T(128)S(1)} all-reduce(f32[2]{0:T(128)S(1)} %get-tuple-element.39), channel_id=1, replica_groups=mesh['dom'=64,'kv'=4] {'dom','kv'}, use_global_device_ids=true, to_apply=%region_20.21 | all-reduce | flops 2 | bytes 16 | tf_op jit(solution)/shard_map/psum | solution.py:184
  1318.3 73.5 %psum.100 = f32[2]{0:T(128)S(1)} all-reduce(f32[2]{0:T(128)S(1)} %get-tuple-element.13), channel_id=1, replica_groups=mesh['dom'=64,'kv'=4] {'dom','kv'}, use_global_device_ids=true, to_apply=%region_22.23 | all-reduce | flops 2 | bytes 16 | tf_op jit(solution)/shard_map/psum | solution.py:111
  1391.8 13.6 fusion.59
  1405.4 245.9 %all-reduce.13.cloned.1.call-done = f32[2,32768]{1,0:T(2,128)} async-done(((f32[2,32768]{1,0:T(2,128)}), f32[2,32768]{1,0:T(2,128)}) %all-reduce.13.cloned.1.call-update) | async-done | bytes 262160 | tf_op jit(solution)/shard_map/psum | solution.py:175
  1651.3 17.1 fusion.5
  1668.4 77.4 %psum.102 = f32[2]{0:T(128)S(1)} all-reduce(f32[2]{0:T(128)S(1)} %fusion.5), channel_id=1, replica_groups=mesh['dom'=64,'kv'=4] {'dom','kv'}, use_global_device_ids=true, to_apply=%region_25.26 | all-reduce | flops 2 | bytes 16 | tf_op jit(solution)/shard_map/psum | solution.py:184
  1745.8 0.2 fusion.62
  1746.0 73.2 %psum.103 = f32[2]{0:T(128)S(1)} all-reduce(f32[2]{0:T(128)S(1)} %get-tuple-element.11), channel_id=1, replica_groups=mesh['dom'=64,'kv'=4] {'dom','kv'}, use_global_device_ids=true, to_apply=%region_27.28 | all-reduce | flops 2 | bytes 16 | tf_op jit(solution)/shard_map/psum | solution.py:192
  1819.3 0.6 fusion.66
  1821.2 0.5 subtract_bitcast_fusion
  (71 shorter events, 2.7 us)
Async XLA Ops:
  7.2 93.3 %copy-start = (bf16[384,128]{1,0:T(8,128)(2,1)S(1)}, bf16[384,128]{1,0:T(8,128)(2,1)}, u32[]{:S(2)}) copy-start(bf16[384,128]{1,0:T(8,128)(2,1)} %param.24) | copy-start | bytes 294916
  7.2 361.2 %all-reduce.7.cloned.1.call-start = ((), (), s32[]{:S(2)}) async-start(), calls=%async_computation | async-start | bytes 524288 | tf_op jit(solution)/shard_map/psum | solution.py:175
  10.0 72.5 %collective-permute-start.2 = (bf16[32,128]{1,0:T(8,128)(2,1)S(1)}, bf16[32,128]{1,0:T(8,128)(2,1)S(1)}, u32[]{:S(2)}, u32[]{:S(2)}) collective-permute-start(bf16[32,128]{1,0:T(8,128)(2,1)S(1)} %get-tuple-element.29), channel_id=1, source_target_pairs={{0,1},{1,2},{2,3},{3,4},{4,5},{5,6},{6,7},{7,8},{8,9},{9,10},{10,1... | collective-permute-start | bytes 24584 | tf_op jit(solution)/shard_map/ppermute | solution.py:20
  12.1 70.4 %collective-permute-start.3 = (bf16[32,128]{1,0:T(8,128)(2,1)S(1)}, bf16[32,128]{1,0:T(8,128)(2,1)S(1)}, u32[]{:S(2)}, u32[]{:S(2)}) collective-permute-start(bf16[32,128]{1,0:T(8,128)(2,1)S(1)} %get-tuple-element.30), channel_id=1, source_target_pairs={{1,0},{2,1},{3,2},{4,3},{5,4},{6,5},{7,6},{8,7},{9,8},{10,9},{11,1... | collective-permute-start | bytes 24584 | tf_op jit(solution)/shard_map/ppermute | solution.py:23
  15.5 43.0 %collective-permute-start = (f32[32,3]{1,0:T(8,128)S(1)}, f32[32,3]{1,0:T(8,128)S(1)}, u32[]{:S(2)}, u32[]{:S(2)}) collective-permute-start(f32[32,3]{1,0:T(8,128)S(1)} %get-tuple-element.27), channel_id=1, source_target_pairs={{0,1},{1,2},{2,3},{3,4},{4,5},{5,6},{6,7},{7,8},{8,9},{9,10},{10,1... | collective-permute-start | bytes 1160 | tf_op jit(solution)/shard_map/ppermute | solution.py:20
  15.6 42.9 %collective-permute-start.1 = (f32[32,3]{1,0:T(8,128)S(1)}, f32[32,3]{1,0:T(8,128)S(1)}, u32[]{:S(2)}, u32[]{:S(2)}) collective-permute-start(f32[32,3]{1,0:T(8,128)S(1)} %get-tuple-element.28), channel_id=1, source_target_pairs={{1,0},{2,1},{3,2},{4,3},{5,4},{6,5},{7,6},{8,7},{9,8},{10,9},{11,1... | collective-permute-start | bytes 1160 | tf_op jit(solution)/shard_map/ppermute | solution.py:23
  58.4 16.8 copy-start.3
  58.4 16.8 copy-start.4
  75.2 7.4 copy-start.2
  82.7 17.8 copy-start.1
  82.7 17.8 copy-start.5
  100.8 13.9 copy-start.6
  114.7 681.3 %all-reduce.9.cloned.1.call-start = ((), (), s32[]{:S(2)}) async-start(), calls=%async_computation.1 | async-start | bytes 524288 | tf_op jit(solution)/shard_map/psum | solution.py:175
  550.1 673.5 %all-reduce.11.cloned.1.call-start = ((), (), s32[]{:S(2)}) async-start(), calls=%async_computation.2 | async-start | bytes 524288 | tf_op jit(solution)/shard_map/psum | solution.py:175
  977.7 673.6 %all-reduce.13.cloned.1.call-start = ((), (), s32[]{:S(2)}) async-start(), calls=%async_computation.3 | async-start | bytes 524288 | tf_op jit(solution)/shard_map/psum | solution.py:175
Sparse Core Ops, SparseCore 0:
  114.9 253.4 all-reduce.6
  550.2 245.7 all-reduce.8
  977.8 245.8 all-reduce.10
  1405.6 245.7 all-reduce.12
where the time goes:
time: 1830 us
  waiting for transfers between devices  991 us (54%)
  blocking collectives  604 us (33%)
  matrix products  127 us (7%)
  other arithmetic  51.7 us (3%)
  local copies, waits for them, and re-layouts  31.7 us (2%)
    psum x4, waiting for transfers between devices, local(): summed = lax.psum(partial_value, ('dom', 'kv'))  991 us
    psum x4, blocking collectives, squares(): return lax.psum(jnp.sum(residual * residual, axis=1), ('dom', 'kv'))  298 us
    psum x3, blocking collectives, local(): curvature = lax.psum(jnp.sum(direction * applied, axis=1), ('dom', 'kv'))  232 us
    psum x1, blocking collectives, local(): totals = lax.psum(jnp.sum(solution, axis=1), ('dom', 'kv'))  73.2 us
    dot_general x4, matrix products, local(): lax.dot_general(summed * weight_pair, phase_table, (((1,), (1,)), ((), ()...  67.8 us
    dot_general x4, matrix products, local(): jnp.dot(direction, phase_table, precision=highest, preferred_element_type...  54.7 us
  transfers between devices with their start and end apart: 8, of which 4 were waited for; matrix products, arithmetic and copies ran while one was open for 4% of the time, Pallas kernels for 0%

commit v1 on v0

--- a/solution.py
+++ b/solution.py
@@ -181,7 +181,8 @@
             preferred_element_type=jnp.float32,
         )
         applied = hardness * direction + potential
-        curvature = lax.psum(jnp.sum(direction * applied, axis=1), ("dom", "kv"))
+        one_axis = lax.psum(jnp.sum(direction * applied, axis=1), "dom")
+        curvature = lax.psum(one_axis, "kv")
         step_size = norm_now / curvature
         solution = solution + step_size[:, None] * direction
         residual = residual - step_size[:, None] * applied

time: 1830 us -> 2140 us (1.17)
  blocking collectives: 604 us -> 916 us
    psum x3 -> x8, blocking collectives: 232 us -> 536 us  [the longest x4 501 us: local(): one_axis = lax.psum(jnp.sum(direction * applied, axis=1), 'dom')]
  transfers between devices with their start and end apart: 8 -> 8, of which waited for: 4 -> 4; matrix products, arithmetic and copies ran while one was open for 4% -> 3% of each run, Pallas kernels for 0% -> 0%
where the time goes in v1:
time: 2140 us
  waiting for transfers between devices  987 us (46%)
  blocking collectives  916 us (43%)
  matrix products  127 us (6%)
  other arithmetic  51.7 us (2%)
  local copies, waits for them, and re-layouts  31.7 us (1%)
    psum x4, waiting for transfers between devices, local(): summed = lax.psum(partial_value, ('dom', 'kv'))  986 us
    psum x4, blocking collectives, local(): one_axis = lax.psum(jnp.sum(direction * applied, axis=1), 'dom')  501 us
    psum x4, blocking collectives, squares(): return lax.psum(jnp.sum(residual * residual, axis=1), ('dom', 'kv'))  305 us
    psum x1, blocking collectives, local(): totals = lax.psum(jnp.sum(solution, axis=1), ('dom', 'kv'))  76.4 us
    dot_general x4, matrix products, local(): lax.dot_general(summed * weight_pair, phase_table, (((1,), (1,)), ((), ()...  67.8 us
    dot_general x4, matrix products, local(): jnp.dot(direction, phase_table, precision=highest, preferred_element_type...  54.7 us
  transfers between devices with their start and end apart: 8, of which 4 were waited for; matrix products, arithmetic and copies ran while one was open for 3% of the time, Pallas kernels for 0%

profile of v1, /device:TPU:1, one launch (start us, length us, event | category | flops | bytes accessed | tf_op | source)
XLA Modules:
  0.0 2137.0 jit_solution(16253367701308560451)
XLA Ops:
  7.2 0.7 compare_and_fusion.2
  7.9 0.7 fusion.49
  8.6 1.4 gather_fusion.2
  10.0 2.1 collective-permute-start.2
  12.1 1.9 collective-permute-start.3
  14.1 0.8 copy.50
  15.6 3.1 collective-permute-start.1
  18.8 0.8 slice_bitcast_fusion.2
  19.6 0.7 compare_and_fusion
  20.3 0.8 copy.48
  21.3 0.9 convolution_convert_fusion
  22.2 0.7 fusion.35
  23.0 1.6 multiply_divide_fusion
  24.6 0.8 select_reduce_fusion
  25.4 33.0 %fusion.1 = (f32[128,16384]{1,0:T(8,128)}, f32[128,16384]{1,0:T(8,128)}) fusion(f32[16384]{0:T(1024)S(1)} %bitcast.46, f32[128]{0:T(128)S(1)} %get-tuple-element.30, f32[16384]{0:T(1024)S(1)} %bitcast.47, f32[128]{0:T(128)S(1)} %get-tuple-element.31, f32[16384]{0:T(1024)S(1)} %bitcast.45, f32[128]{0:T(128)S(1)} %get-tuple-element.29), kind=kLoop, calls=%fused_computation.7 | loop fusion | flops 12582912 | bytes 16975360 | tf_op jit(solution)/shard_map/cos | solution.py:45
  58.5 10.8 gather_fusion.1
  69.3 2.1 select_bitcast_fusion
  71.5 2.8 slice_reduce_fusion.2
  75.2 3.3 fusion.3
  78.5 3.9 broadcast_multiply_fusion
  82.7 12.1 gather_fusion.3
  94.9 3.3 fusion.2
  98.2 2.2 multiply_reduce_fusion
  100.8 13.9 fusion.41
  114.8 253.6 %all-reduce.6.cloned.1.call-done = f32[2,32768]{1,0:T(2,128)} async-done(((f32[2,32768]{1,0:T(2,128)}), f32[2,32768]{1,0:T(2,128)}) %all-reduce.6.cloned.1.call-update) | async-done | bytes 262160 | tf_op jit(solution)/shard_map/psum | solution.py:175
  368.4 16.8 fusion.44
  385.2 125.3 %psum.121 = f32[2]{0:T(128)S(1)} all-reduce(f32[2]{0:T(128)S(1)} %get-tuple-element.5), channel_id=1, replica_groups=mesh['dom'=64,'kv'=4] {'dom'}, use_global_device_ids=true, to_apply=%region_10.11 | all-reduce | flops 2 | bytes 16 | tf_op jit(solution)/shard_map/psum | solution.py:184
  510.5 8.5 psum.122
  519.1 76.8 %psum.119 = f32[2]{0:T(128)S(1)} all-reduce(f32[2]{0:T(128)S(1)} %get-tuple-element.6), channel_id=1, replica_groups=mesh['dom'=64,'kv'=4] {'dom','kv'}, use_global_device_ids=true, to_apply=%region_6.7 | all-reduce | flops 2 | bytes 16 | tf_op jit(solution)/shard_map/psum | solution.py:111
  596.1 74.5 %psum.123 = f32[2]{0:T(128)S(1)} all-reduce(f32[2]{0:T(128)S(1)} %get-tuple-element.15), channel_id=1, replica_groups=mesh['dom'=64,'kv'=4] {'dom','kv'}, use_global_device_ids=true, to_apply=%region_13.14 | all-reduce | flops 2 | bytes 16 | tf_op jit(solution)/shard_map/psum | solution.py:111
  670.6 13.6 fusion.61
  684.3 244.3 %all-reduce.8.cloned.1.call-done = f32[2,32768]{1,0:T(2,128)} async-done(((f32[2,32768]{1,0:T(2,128)}), f32[2,32768]{1,0:T(2,128)}) %all-reduce.8.cloned.1.call-update) | async-done | bytes 262160 | tf_op jit(solution)/shard_map/psum | solution.py:175
  928.5 16.9 multiply_reduce_fusion.6
  945.5 125.3 %psum.125 = f32[2]{0:T(128)S(1)} all-reduce(f32[2]{0:T(128)S(1)} %get-tuple-element.35), channel_id=1, replica_groups=mesh['dom'=64,'kv'=4] {'dom'}, use_global_device_ids=true, to_apply=%region_16.17 | all-reduce | flops 2 | bytes 16 | tf_op jit(solution)/shard_map/psum | solution.py:184
  1070.8 8.5 psum.126
  1079.5 76.6 %psum.127 = f32[2]{0:T(128)S(1)} all-reduce(f32[2]{0:T(128)S(1)} %get-tuple-element.13), channel_id=1, replica_groups=mesh['dom'=64,'kv'=4] {'dom','kv'}, use_global_device_ids=true, to_apply=%region_19.20 | all-reduce | flops 2 | bytes 16 | tf_op jit(solution)/shard_map/psum | solution.py:111
  1156.2 13.6 fusion.60
  1169.9 244.4 %all-reduce.10.cloned.1.call-done = f32[2,32768]{1,0:T(2,128)} async-done(((f32[2,32768]{1,0:T(2,128)}), f32[2,32768]{1,0:T(2,128)}) %all-reduce.10.cloned.1.call-update) | async-done | bytes 262160 | tf_op jit(solution)/shard_map/psum | solution.py:175
  1414.2 17.0 multiply_reduce_fusion.4
  1431.2 125.3 %psum.129 = f32[2]{0:T(128)S(1)} all-reduce(f32[2]{0:T(128)S(1)} %get-tuple-element.37), channel_id=1, replica_groups=mesh['dom'=64,'kv'=4] {'dom'}, use_global_device_ids=true, to_apply=%region_22.23 | all-reduce | flops 2 | bytes 16 | tf_op jit(solution)/shard_map/psum | solution.py:184
  1556.6 8.5 psum.130
  1565.3 76.7 %psum.131 = f32[2]{0:T(128)S(1)} all-reduce(f32[2]{0:T(128)S(1)} %get-tuple-element.11), channel_id=1, replica_groups=mesh['dom'=64,'kv'=4] {'dom','kv'}, use_global_device_ids=true, to_apply=%region_25.26 | all-reduce | flops 2 | bytes 16 | tf_op jit(solution)/shard_map/psum | solution.py:111
  1642.0 13.6 fusion.59
  1655.6 244.3 %all-reduce.12.cloned.1.call-done = f32[2,32768]{1,0:T(2,128)} async-done(((f32[2,32768]{1,0:T(2,128)}), f32[2,32768]{1,0:T(2,128)}) %all-reduce.12.cloned.1.call-update) | async-done | bytes 262160 | tf_op jit(solution)/shard_map/psum | solution.py:175
  1899.9 17.1 fusion.5
  1916.9 125.3 %psum.133 = f32[2]{0:T(128)S(1)} all-reduce(f32[2]{0:T(128)S(1)} %fusion.5), channel_id=1, replica_groups=mesh['dom'=64,'kv'=4] {'dom'}, use_global_device_ids=true, to_apply=%region_28.29 | all-reduce | flops 2 | bytes 16 | tf_op jit(solution)/shard_map/psum | solution.py:184
  2042.3 8.5 psum.134
  2051.0 76.4 %psum.135 = f32[2]{0:T(128)S(1)} all-reduce(f32[2]{0:T(128)S(1)} %get-tuple-element.9), channel_id=1, replica_groups=mesh['dom'=64,'kv'=4] {'dom','kv'}, use_global_device_ids=true, to_apply=%region_31.32 | all-reduce | flops 2 | bytes 16 | tf_op jit(solution)/shard_map/psum | solution.py:193
  (76 shorter events, 4.9 us)
Async XLA Ops:
  7.2 93.3 %copy-start = (bf16[384,128]{1,0:T(8,128)(2,1)S(1)}, bf16[384,128]{1,0:T(8,128)(2,1)}, u32[]{:S(2)}) copy-start(bf16[384,128]{1,0:T(8,128)(2,1)} %param.24) | copy-start | bytes 294916
  7.2 361.2 %all-reduce.6.cloned.1.call-start = ((), (), s32[]{:S(2)}) async-start(), calls=%async_computation | async-start | bytes 524288 | tf_op jit(solution)/shard_map/psum | solution.py:175
  10.0 72.5 %collective-permute-start.2 = (bf16[32,128]{1,0:T(8,128)(2,1)S(1)}, bf16[32,128]{1,0:T(8,128)(2,1)S(1)}, u32[]{:S(2)}, u32[]{:S(2)}) collective-permute-start(bf16[32,128]{1,0:T(8,128)(2,1)S(1)} %get-tuple-element.27), channel_id=1, source_target_pairs={{0,1},{1,2},{2,3},{3,4},{4,5},{5,6},{6,7},{7,8},{8,9},{9,10},{10,1... | collective-permute-start | bytes 24584 | tf_op jit(solution)/shard_map/ppermute | solution.py:20
  12.1 70.4 %collective-permute-start.3 = (bf16[32,128]{1,0:T(8,128)(2,1)S(1)}, bf16[32,128]{1,0:T(8,128)(2,1)S(1)}, u32[]{:S(2)}, u32[]{:S(2)}) collective-permute-start(bf16[32,128]{1,0:T(8,128)(2,1)S(1)} %get-tuple-element.28), channel_id=1, source_target_pairs={{1,0},{2,1},{3,2},{4,3},{5,4},{6,5},{7,6},{8,7},{9,8},{10,9},{11,1... | collective-permute-start | bytes 24584 | tf_op jit(solution)/shard_map/ppermute | solution.py:23
  15.5 43.0 %collective-permute-start = (f32[32,3]{1,0:T(8,128)S(1)}, f32[32,3]{1,0:T(8,128)S(1)}, u32[]{:S(2)}, u32[]{:S(2)}) collective-permute-start(f32[32,3]{1,0:T(8,128)S(1)} %get-tuple-element.25), channel_id=1, source_target_pairs={{0,1},{1,2},{2,3},{3,4},{4,5},{5,6},{6,7},{7,8},{8,9},{9,10},{10,1... | collective-permute-start | bytes 1160 | tf_op jit(solution)/shard_map/ppermute | solution.py:20
  15.6 42.9 %collective-permute-start.1 = (f32[32,3]{1,0:T(8,128)S(1)}, f32[32,3]{1,0:T(8,128)S(1)}, u32[]{:S(2)}, u32[]{:S(2)}) collective-permute-start(f32[32,3]{1,0:T(8,128)S(1)} %get-tuple-element.26), channel_id=1, source_target_pairs={{1,0},{2,1},{3,2},{4,3},{5,4},{6,5},{7,6},{8,7},{9,8},{10,9},{11,1... | collective-permute-start | bytes 1160 | tf_op jit(solution)/shard_map/ppermute | solution.py:23
  58.4 16.8 copy-start.3
  58.4 16.8 copy-start.4
  75.2 7.4 copy-start.2
  82.7 17.8 copy-start.1
  82.7 17.8 copy-start.5
  100.8 13.9 copy-start.6
  114.7 813.8 %all-reduce.8.cloned.1.call-start = ((), (), s32[]{:S(2)}) async-start(), calls=%async_computation.1 | async-start | bytes 524288 | tf_op jit(solution)/shard_map/psum | solution.py:175
  684.2 730.0 %all-reduce.10.cloned.1.call-start = ((), (), s32[]{:S(2)}) async-start(), calls=%async_computation.2 | async-start | bytes 524288 | tf_op jit(solution)/shard_map/psum | solution.py:175
  1169.8 730.0 %all-reduce.12.cloned.1.call-start = ((), (), s32[]{:S(2)}) async-start(), calls=%async_computation.3 | async-start | bytes 524288 | tf_op jit(solution)/shard_map/psum | solution.py:175
Sparse Core Ops, SparseCore 0:
  114.9 253.4 all-reduce.5
  684.3 244.1 all-reduce.7
  1169.9 244.2 all-reduce.9
  1655.7 244.0 all-reduce.11
